TPU v7x, 32 devices: a whole 2x2x4 slice. The times are simulated.
32 devices in a mesh: cases: 2 (over y), circ: 4 (over z), width: 4 (over x, core).
Axes of the slice: x: 2, y: 2, z: 4, core: 2. Of those that a mesh axis runs over, the one named last changes fastest.
Arguments:
- forcing: float32 [3, 12, 64, 512], P(None, 'cases', 'width', 'circ'), parts along dimension 1, may hold values from -120 to 120
- case_ids: int32 [2], P('cases'), parts along dimension 0, may hold values from 0 to 15
- load_gain: float32 [16, 3], replicated, may hold values from 0.1 to 1.9
- stiffness: float32 [6, 64, 512], P(None, 'width', 'circ'), may hold values from 0.6 to 1.6
- convection: float32 [6, 64, 512], P(None, 'width', 'circ'), may hold values from 0.5 to 3
- labels: int32 [6, 64], P(None, 'width'), may hold values from 0 to 7
- zone_diagonal: float32 [8, 3, 3], replicated, may hold values from -2 to 2
- zone_coupling: float32 [8, 6, 3, 3], replicated, may hold values from -0.25 to 0.75
- zone_jacobi: float32 [8, 3, 3], replicated, may hold values from -0.03 to 0.18
- coarse_inverse: float32 [12, 12], replicated, may hold values from -4.0690104e-07 to 8.138021e-06
Outputs:
- adjoint_field: float32 [3, 12, 64, 512], P(None, 'cases', 'width', 'circ'), parts along dimension 1
- adjoint_residual: float32 [3, 12, 64, 512], P(None, 'cases', 'width', 'circ'), parts along dimension 1
There are 2 independent parts, one for each index of `cases`. A program takes and returns all parts, laid end to end along the dimension named above; an argument that names none is the same for every part. Nothing has to cross between parts.
All inputs are finite; a program needn't handle non-finite values.
Results may differ from a plain program's by a relative error of at most 0.0003.
Values sent between devices are 32-bit elements; how exact they have to be, the bound alone decides.
A program may use at most 64 MiB of HBM per device.

v0:
```python
import jax
import jax.numpy as jnp
from jax import lax
from jax.sharding import PartitionSpec as P

ITERS = 4


highest = lax.Precision.HIGHEST


def shifted(value, axis, steps):
    count = lax.axis_size(axis)
    pairs = [(source, (source + steps) % count) for source in range(count)]
    return lax.ppermute(value, axis, pairs)


def from_behind_2(x, axis, by):
    size = lax.axis_size(axis)
    pairs = [(i, i + by) for i in range(size) if 0 <= i + by < size]
    return lax.ppermute(x, axis, pairs)


def shift_down(values, axis):
    widths = [(0, 0)] * values.ndim
    widths[axis] = (1, 0)
    padded = jnp.pad(values, widths)
    return lax.slice_in_dim(padded, 0, values.shape[axis], axis=axis)


def shift_up(values, axis):
    widths = [(0, 0)] * values.ndim
    widths[axis] = (0, 1)
    padded = jnp.pad(values, widths)
    return lax.slice_in_dim(padded, 1, values.shape[axis] + 1, axis=axis)


def zone_fields(labels, zone_diagonal, zone_coupling, zone_jacobi):
    zone_count = zone_coupling.shape[0]
    onehot = (labels[None, :, :] == jnp.arange(zone_count, dtype=jnp.int32)[:, None, None]).astype(
        jnp.float32
    )
    coupling = jnp.einsum("zdba,zrw->dbarw", zone_coupling, onehot, precision=highest)
    diagonal = jnp.einsum("zba,zrw->barw", zone_diagonal, onehot, precision=highest)
    jacobi = jnp.einsum("zab,zrw->abrw", zone_jacobi, onehot, precision=highest)
    return (coupling, diagonal, jacobi)


def transposed(vector, stiffness, convection, coupling, diagonal):
    contrib = [
        stiffness * jnp.einsum("barw,brwc->arwc", coupling[d], vector, precision=highest)
        for d in range(6)
    ]
    halfway = 0.5 * convection
    contrib[0] = contrib[0] - halfway * vector
    contrib[1] = contrib[1] + halfway * vector
    result = stiffness * (
        7.0 * vector + jnp.einsum("barw,brwc->arwc", diagonal, vector, precision=highest)
    )
    from_ahead = shifted(contrib[0][:, :, :, -1:], "circ", 1)
    circ_lower = jnp.concatenate([from_ahead, contrib[0][:, :, :, :-1]], axis=3)
    from_behind = shifted(contrib[1][:, :, :, :1], "circ", -1)
    circ_upper = jnp.concatenate([contrib[1][:, :, :, 1:], from_behind], axis=3)
    tread_top = from_behind_2(contrib[2][:, :, -1:, :], "width", 1)
    tread_lower = jnp.concatenate([tread_top, contrib[2][:, :, :-1, :]], axis=2)
    tread_bottom = from_behind_2(contrib[3][:, :, :1, :], "width", -1)
    tread_upper = jnp.concatenate([contrib[3][:, :, 1:, :], tread_bottom], axis=2)
    moved = [
        circ_lower,
        circ_upper,
        tread_lower,
        tread_upper,
        shift_down(contrib[4], 1),
        shift_up(contrib[5], 1),
    ]
    for piece in moved:
        result = result - piece
    return result


def coarse_sums(vector):
    local_totals = jnp.sum(vector, axis=(1, 2, 3))
    sector_sum = lax.psum(local_totals, "width")
    return lax.all_gather(sector_sum[None, :], "circ", axis=0, tiled=True)


def precondition(vector, stiffness, jacobi, coarse_inverse, all_sectors):
    position = lax.axis_index("circ")
    own_rows = lax.dynamic_slice_in_dim(coarse_inverse, position * 3, 3, 0)
    correction = jnp.dot(own_rows, all_sectors.reshape(-1), precision=highest)
    local_part = jnp.einsum("abrw,brwc->arwc", jacobi, vector, precision=highest) / stiffness
    return local_part + correction[:, None, None, None]


def least_squares(start_size, hessen):
    count = len(hessen)
    rotated = [start_size] + [jnp.zeros((), start_size.dtype) for spare in range(count)]
    rotations = []
    triangle = []
    for j in range(count):
        column = list(hessen[j])
        for i in range(j):
            cosine, sine_value = rotations[i]
            top_entry = column[i]
            low_entry = column[i + 1]
            column[i] = cosine * top_entry + sine_value * low_entry
            column[i + 1] = cosine * low_entry - sine_value * top_entry
        radius = jnp.sqrt(column[j] * column[j] + column[j + 1] * column[j + 1])
        cosine = column[j] / radius
        sine_value = column[j + 1] / radius
        rotations.append((cosine, sine_value))
        column[j] = radius
        carried = rotated[j]
        rotated[j] = cosine * carried
        rotated[j + 1] = -sine_value * carried
        triangle.append(column[: j + 1])
    weights = [None] * count
    for j in reversed(range(count)):
        remainder = rotated[j]
        for k in range(j + 1, count):
            remainder = remainder - triangle[k][j] * weights[k]
        weights[j] = remainder / triangle[j][j]
    return weights


def on_device(
    forcing,
    case_ids,
    load_gain,
    stiffness,
    convection,
    labels,
    zone_diagonal,
    zone_coupling,
    zone_jacobi,
    coarse_inverse,
):
    selector = (jnp.arange(load_gain.shape[0], dtype=jnp.int32) == case_ids[0]).astype(jnp.float32)
    load_row = jnp.sum(selector[:, None] * load_gain, axis=0)
    right_side = forcing * load_row[:, None, None, None]
    coupling, diagonal, jacobi = zone_fields(labels, zone_diagonal, zone_coupling, zone_jacobi)
    start_size = jnp.sqrt(lax.psum(jnp.sum(right_side * right_side), ("circ", "width")))
    krylov = [right_side / start_size]
    hessen = []
    for j in range(ITERS):
        current_sums = coarse_sums(krylov[j])
        candidate = transposed(
            precondition(krylov[j], stiffness, jacobi, coarse_inverse, current_sums),
            stiffness,
            convection,
            coupling,
            diagonal,
        )
        heights = []
        for i in range(j + 1):
            height = lax.psum(jnp.sum(krylov[i] * candidate), ("circ", "width"))
            heights.append(height)
            candidate = candidate - height * krylov[i]
        new_height = jnp.sqrt(lax.psum(jnp.sum(candidate * candidate), ("circ", "width")))
        hessen.append(heights + [new_height])
        if j + 1 < ITERS:
            krylov.append(candidate / new_height)
    weights = least_squares(start_size, hessen)
    combined = weights[0] * krylov[0]
    for j in range(1, ITERS):
        combined = combined + weights[j] * krylov[j]
    combined_sums = coarse_sums(combined)
    adjoint_field = precondition(combined, stiffness, jacobi, coarse_inverse, combined_sums)
    adjoint_residual = right_side - transposed(
        adjoint_field, stiffness, convection, coupling, diagonal
    )
    return (adjoint_field, adjoint_residual)


def solution(mesh):
    return jax.shard_map(
        on_device,
        mesh=mesh,
        in_specs=(
            P(None, "cases", "width", "circ"),
            P("cases"),
            P(),
            P(None, "width", "circ"),
            P(None, "width", "circ"),
            P(None, "width"),
            P(),
            P(),
            P(),
            P(),
        ),
        out_specs=(P(None, "cases", "width", "circ"), P(None, "cases", "width", "circ")),
        check_vma=False,
    )
```

profile of v0, /device:TPU:0, one launch (start us, length us, event | category | flops | bytes accessed | tf_op | source)
XLA Modules:
  0.0 677.0 jit_solution(62090292536471604)
XLA Ops:
  2.1 1.7 multiply_reduce_fusion.14
  3.8 35.5 %psum.140 = f32[]{:T(128)} all-reduce(f32[]{:T(128)} %multiply_reduce_fusion.14), channel_id=1, replica_groups=mesh['cases'=2,'circ'=4,'width'=4] {'circ','width'}, use_global_device_ids=true, to_apply=%region_2.0 | all-reduce | flops 1 | bytes 8 | tf_op jit(solution)/shard_map/psum | solution.py:142
  40.3 5.8 psum.141
  46.1 7.5 %all-gather = f32[4,1,3]{2,1,0:T(1,128)S(1)} all-gather(f32[1,1,3]{2,1,0:T(1,128)S(1)} %bitcast.322), channel_id=1, replica_groups=mesh['cases'=2,'circ'=4,'width'=4] {'circ'}, dimensions={0}, use_global_device_ids=true | all-gather | bytes 60 | tf_op jit(solution)/shard_map/all_gather | solution.py:84
  59.7 2.1 collective-permute-start
  62.8 1.9 collective-permute-start.1
  74.5 3.0 multiply_reduce_fusion.13
  77.5 31.8 %psum.142 = f32[]{:T(128)} all-reduce(f32[]{:T(128)} %get-tuple-element.30), channel_id=1, replica_groups=mesh['cases'=2,'circ'=4,'width'=4] {'circ','width'}, use_global_device_ids=true, to_apply=%region_6.7 | all-reduce | flops 1 | bytes 8 | tf_op jit(solution)/shard_map/psum | solution.py:156
  110.7 30.2 %psum.143 = f32[]{:T(128)} all-reduce(f32[]{:T(128)} %multiply_reduce_fusion.12), channel_id=1, replica_groups=mesh['cases'=2,'circ'=4,'width'=4] {'circ','width'}, use_global_device_ids=true, to_apply=%region_8.9 | all-reduce | flops 1 | bytes 8 | tf_op jit(solution)/shard_map/psum | solution.py:159
  142.5 5.8 psum.144
  148.2 8.0 %all-gather.1 = f32[4,1,3]{2,1,0:T(1,128)S(1)} all-gather(f32[1,1,3]{2,1,0:T(1,128)S(1)} %bitcast.323), channel_id=1, replica_groups=mesh['cases'=2,'circ'=4,'width'=4] {'circ'}, dimensions={0}, use_global_device_ids=true | all-gather | bytes 60 | tf_op jit(solution)/shard_map/all_gather | solution.py:84
  161.1 1.5 fusion.37
  162.7 2.1 collective-permute-start.4
  164.7 1.8 collective-permute-start.5
  173.6 3.0 multiply_reduce_fusion.11
  176.6 33.1 %psum.145 = f32[]{:T(128)} all-reduce(f32[]{:T(128)} %get-tuple-element.32), channel_id=1, replica_groups=mesh['cases'=2,'circ'=4,'width'=4] {'circ','width'}, use_global_device_ids=true, to_apply=%region_12.13 | all-reduce | flops 1 | bytes 8 | tf_op jit(solution)/shard_map/psum | solution.py:156
  211.0 30.1 %psum.146 = f32[]{:T(128)} all-reduce(f32[]{:T(128)} %multiply_reduce_fusion.10), channel_id=1, replica_groups=mesh['cases'=2,'circ'=4,'width'=4] {'circ','width'}, use_global_device_ids=true, to_apply=%region_14.15 | all-reduce | flops 1 | bytes 8 | tf_op jit(solution)/shard_map/psum | solution.py:156
  241.2 2.1 multiply_reduce_fusion.9
  243.2 30.1 %psum.147 = f32[]{:T(128)} all-reduce(f32[]{:T(128)} %get-tuple-element.18), channel_id=1, replica_groups=mesh['cases'=2,'circ'=4,'width'=4] {'circ','width'}, use_global_device_ids=true, to_apply=%region_16.17 | all-reduce | flops 1 | bytes 8 | tf_op jit(solution)/shard_map/psum | solution.py:159
  274.2 5.8 psum.148
  279.9 7.7 %all-gather.2 = f32[4,1,3]{2,1,0:T(1,128)S(1)} all-gather(f32[1,1,3]{2,1,0:T(1,128)S(1)} %bitcast.324), channel_id=1, replica_groups=mesh['cases'=2,'circ'=4,'width'=4] {'circ'}, dimensions={0}, use_global_device_ids=true | all-gather | bytes 60 | tf_op jit(solution)/shard_map/all_gather | solution.py:84
  294.7 2.0 collective-permute-start.8
  296.7 1.8 collective-permute-start.9
  306.2 3.0 multiply_reduce_fusion.8
  309.2 33.1 %psum.149 = f32[]{:T(128)} all-reduce(f32[]{:T(128)} %get-tuple-element.34), channel_id=1, replica_groups=mesh['cases'=2,'circ'=4,'width'=4] {'circ','width'}, use_global_device_ids=true, to_apply=%region_20.21 | all-reduce | flops 1 | bytes 8 | tf_op jit(solution)/shard_map/psum | solution.py:156
  343.7 30.2 %psum.150 = f32[]{:T(128)} all-reduce(f32[]{:T(128)} %multiply_reduce_fusion.7), channel_id=1, replica_groups=mesh['cases'=2,'circ'=4,'width'=4] {'circ','width'}, use_global_device_ids=true, to_apply=%region_22.23 | all-reduce | flops 1 | bytes 8 | tf_op jit(solution)/shard_map/psum | solution.py:156
  373.9 2.1 multiply_reduce_fusion.6
  375.9 30.1 %psum.151 = f32[]{:T(128)} all-reduce(f32[]{:T(128)} %get-tuple-element.14), channel_id=1, replica_groups=mesh['cases'=2,'circ'=4,'width'=4] {'circ','width'}, use_global_device_ids=true, to_apply=%region_24.25 | all-reduce | flops 1 | bytes 8 | tf_op jit(solution)/shard_map/psum | solution.py:156
  407.5 30.2 %psum.152 = f32[]{:T(128)} all-reduce(f32[]{:T(128)} %multiply_reduce_fusion.5), channel_id=1, replica_groups=mesh['cases'=2,'circ'=4,'width'=4] {'circ','width'}, use_global_device_ids=true, to_apply=%region_26.27 | all-reduce | flops 1 | bytes 8 | tf_op jit(solution)/shard_map/psum | solution.py:159
  439.2 5.8 psum.153
  445.0 7.7 %all-gather.3 = f32[4,1,3]{2,1,0:T(1,128)S(1)} all-gather(f32[1,1,3]{2,1,0:T(1,128)S(1)} %bitcast.325), channel_id=1, replica_groups=mesh['cases'=2,'circ'=4,'width'=4] {'circ'}, dimensions={0}, use_global_device_ids=true | all-gather | bytes 60 | tf_op jit(solution)/shard_map/all_gather | solution.py:84
  457.5 1.5 fusion.13
  463.9 2.0 collective-permute-start.12
  466.7 1.8 collective-permute-start.13
  473.2 4.6 collective-permute-done.13
  477.8 3.0 multiply_reduce_fusion.4
  480.9 31.4 %psum.154 = f32[]{:T(128)} all-reduce(f32[]{:T(128)} %get-tuple-element.36), channel_id=1, replica_groups=mesh['cases'=2,'circ'=4,'width'=4] {'circ','width'}, use_global_device_ids=true, to_apply=%region_30.31 | all-reduce | flops 1 | bytes 8 | tf_op jit(solution)/shard_map/psum | solution.py:156
  514.3 30.0 %psum.155 = f32[]{:T(128)} all-reduce(f32[]{:T(128)} %multiply_reduce_fusion.3), channel_id=1, replica_groups=mesh['cases'=2,'circ'=4,'width'=4] {'circ','width'}, use_global_device_ids=true, to_apply=%region_32.33 | all-reduce | flops 1 | bytes 8 | tf_op jit(solution)/shard_map/psum | solution.py:156
  544.9 2.0 multiply_reduce_fusion.2
  548.1 30.0 %psum.156 = f32[]{:T(128)} all-reduce(f32[]{:T(128)} %get-tuple-element.10), channel_id=1, replica_groups=mesh['cases'=2,'circ'=4,'width'=4] {'circ','width'}, use_global_device_ids=true, to_apply=%region_34.35 | all-reduce | flops 1 | bytes 8 | tf_op jit(solution)/shard_map/psum | solution.py:156
  580.1 30.0 %psum.157 = f32[]{:T(128)} all-reduce(f32[]{:T(128)} %multiply_reduce_fusion.1), channel_id=1, replica_groups=mesh['cases'=2,'circ'=4,'width'=4] {'circ','width'}, use_global_device_ids=true, to_apply=%region_36.37 | all-reduce | flops 1 | bytes 8 | tf_op jit(solution)/shard_map/psum | solution.py:156
  610.1 2.0 multiply_reduce_fusion
  613.8 30.0 %psum.158 = f32[]{:T(128)} all-reduce(f32[]{:T(128)} %multiply_reduce_fusion), channel_id=1, replica_groups=mesh['cases'=2,'circ'=4,'width'=4] {'circ','width'}, use_global_device_ids=true, to_apply=%region_38.39 | all-reduce | flops 1 | bytes 8 | tf_op jit(solution)/shard_map/psum | solution.py:159
  645.1 5.8 psum.159
  650.8 7.8 %all-gather.4 = f32[4,1,3]{2,1,0:T(1,128)S(1)} all-gather(f32[1,1,3]{2,1,0:T(1,128)S(1)} %bitcast.326), channel_id=1, replica_groups=mesh['cases'=2,'circ'=4,'width'=4] {'circ'}, dimensions={0}, use_global_device_ids=true | all-gather | bytes 60 | tf_op jit(solution)/shard_map/all_gather | solution.py:84
  664.3 2.1 collective-permute-start.16
  666.4 1.8 collective-permute-start.17
  673.3 1.6 collective-permute-done.17
  (167 shorter events, 73.9 us)
Async XLA Ops:
  0.6 55.3 %copy-start = (f32[8,6,3,3]{1,0,3,2:T(8,128)S(1)}, f32[8,6,3,3]{1,0,3,2:T(8,128)}, u32[]{:S(2)}) copy-start(f32[8,6,3,3]{1,0,3,2:T(8,128)} %param.17) | copy-start | bytes 5188
  0.6 39.4 %copy-start.7 = (f32[3,6,16,128]{3,2,1,0:T(8,128)S(1)}, f32[3,6,16,128]{3,2,1,0:T(8,128)}, u32[]{:S(2)}) copy-start(f32[3,6,16,128]{3,2,1,0:T(8,128)} %param.10) | copy-start | bytes 442372
  54.9 0.7 copy-start.11
  54.9 0.7 copy-start.9
  56.4 0.8 copy-start.8
  57.2 0.7 copy-start.10
  57.2 0.8 copy-start.1
  59.7 14.1 %collective-permute-start = (f32[3,6,16,1]{3,0,2,1:T(4,128)S(1)}, f32[3,6,16,1]{3,0,2,1:T(4,128)}, u32[]{:S(2)}, u32[]{:S(2)}) collective-permute-start(f32[3,6,16,1]{3,0,2,1:T(4,128)S(1)} %slice.249), channel_id=1, source_target_pairs={{0,4},{4,8},{8,12},{12,0},{1,5},{5,9},{9,13},{13,1},{2,6},{6,10},{... | collective-permute-start | bytes 3464 | tf_op jit(solution)/shard_map/ppermute | solution.py:15
  62.8 11.0 %collective-permute-start.1 = (f32[3,6,16,1]{3,0,2,1:T(4,128)S(1)}, f32[3,6,16,1]{3,0,2,1:T(4,128)}, u32[]{:S(2)}, u32[]{:S(2)}) collective-permute-start(f32[3,6,16,1]{3,0,2,1:T(4,128)S(1)} %bitcast.317), channel_id=1, source_target_pairs={{0,12},{4,0},{8,4},{12,8},{1,13},{5,1},{9,5},{13,9},{2,14},{6,2},{... | collective-permute-start | bytes 3464 | tf_op jit(solution)/shard_map/ppermute | solution.py:15
  65.6 7.2 %copy-start.5 = (f32[3,6,16,128]{3,0,2,1:T(4,128)}, f32[3,6,16,128]{3,0,2,1:T(4,128)S(1)}, u32[]{:S(2)}) copy-start(f32[3,6,16,128]{3,0,2,1:T(4,128)S(1)} %fusion.51) | copy-start | bytes 442372
  65.6 8.2 %collective-permute-start.2 = (f32[3,6,1,128]{3,0,2,1:T(4,128)S(1)}, f32[3,6,1,128]{3,0,2,1:T(4,128)S(1)}, u32[]{:S(2)}, u32[]{:S(2)}) collective-permute-start(f32[3,6,1,128]{3,0,2,1:T(4,128)S(1)} %slice.255), channel_id=1, source_target_pairs={{0,1},{1,2},{2,3},{4,5},{5,6},{6,7},{8,9},{9,10},{10,11},{12,13},{... | collective-permute-start | bytes 27656 | tf_op jit(solution)/shard_map/ppermute | solution.py:21
  67.9 5.9 collective-permute-start.3
  71.1 1.5 copy-start.12
  73.6 0.9 slice-start.3
  160.3 10.5 %copy-start.3 = (f32[3,6,16,128]{3,0,2,1:T(4,128)}, f32[3,6,16,128]{3,0,2,1:T(4,128)S(1)}, u32[]{:S(2)}) copy-start(f32[3,6,16,128]{3,0,2,1:T(4,128)S(1)} %fusion.39) | copy-start | bytes 442372
  162.7 10.9 %collective-permute-start.4 = (f32[3,6,16,1]{3,0,2,1:T(4,128)S(1)}, f32[3,6,16,1]{3,0,2,1:T(4,128)}, u32[]{:S(2)}, u32[]{:S(2)}) collective-permute-start(f32[3,6,16,1]{3,0,2,1:T(4,128)S(1)} %slice.262), channel_id=1, source_target_pairs={{0,4},{4,8},{8,12},{12,0},{1,5},{5,9},{9,13},{13,1},{2,6},{6,10},{... | collective-permute-start | bytes 3464 | tf_op jit(solution)/shard_map/ppermute | solution.py:15
  164.7 8.8 %collective-permute-start.5 = (f32[3,6,16,1]{3,0,2,1:T(4,128)S(1)}, f32[3,6,16,1]{3,0,2,1:T(4,128)}, u32[]{:S(2)}, u32[]{:S(2)}) collective-permute-start(f32[3,6,16,1]{3,0,2,1:T(4,128)S(1)} %bitcast.316), channel_id=1, source_target_pairs={{0,12},{4,0},{8,4},{12,8},{1,13},{5,1},{9,5},{13,9},{2,14},{6,2},{... | collective-permute-start | bytes 3464 | tf_op jit(solution)/shard_map/ppermute | solution.py:15
  166.6 7.0 %collective-permute-start.6 = (f32[3,6,1,128]{3,0,2,1:T(4,128)S(1)}, f32[3,6,1,128]{3,0,2,1:T(4,128)S(1)}, u32[]{:S(2)}, u32[]{:S(2)}) collective-permute-start(f32[3,6,1,128]{3,0,2,1:T(4,128)S(1)} %slice.266), channel_id=1, source_target_pairs={{0,1},{1,2},{2,3},{4,5},{5,6},{6,7},{8,9},{9,10},{10,11},{12,13},{... | collective-permute-start | bytes 27656 | tf_op jit(solution)/shard_map/ppermute | solution.py:21
  167.9 5.7 collective-permute-start.7
  170.8 2.8 slice-start.1
  291.6 11.1 %copy-start.4 = (f32[3,6,16,128]{3,0,2,1:T(4,128)}, f32[3,6,16,128]{3,0,2,1:T(4,128)S(1)}, u32[]{:S(2)}) copy-start(f32[3,6,16,128]{3,0,2,1:T(4,128)S(1)} %fusion.27) | copy-start | bytes 442372
  294.7 11.5 %collective-permute-start.8 = (f32[3,6,16,1]{3,0,2,1:T(4,128)}, f32[3,6,16,1]{3,0,2,1:T(4,128)}, u32[]{:S(2)}, u32[]{:S(2)}) collective-permute-start(f32[3,6,16,1]{3,0,2,1:T(4,128)} %slice.270), channel_id=1, source_target_pairs={{0,4},{4,8},{8,12},{12,0},{1,5},{5,9},{9,13},{13,1},{2,6},{6,10},{... | collective-permute-start | bytes 3464 | tf_op jit(solution)/shard_map/ppermute | solution.py:15
  296.7 9.5 %collective-permute-start.9 = (f32[3,6,16,1]{3,0,2,1:T(4,128)S(1)}, f32[3,6,16,1]{3,0,2,1:T(4,128)}, u32[]{:S(2)}, u32[]{:S(2)}) collective-permute-start(f32[3,6,16,1]{3,0,2,1:T(4,128)S(1)} %bitcast.315), channel_id=1, source_target_pairs={{0,12},{4,0},{8,4},{12,8},{1,13},{5,1},{9,5},{13,9},{2,14},{6,2},{... | collective-permute-start | bytes 3464 | tf_op jit(solution)/shard_map/ppermute | solution.py:15
  298.5 7.7 %collective-permute-start.10 = (f32[3,6,1,128]{3,0,2,1:T(4,128)S(1)}, f32[3,6,1,128]{3,0,2,1:T(4,128)S(1)}, u32[]{:S(2)}, u32[]{:S(2)}) collective-permute-start(f32[3,6,1,128]{3,0,2,1:T(4,128)S(1)} %slice.274), channel_id=1, source_target_pairs={{0,1},{1,2},{2,3},{4,5},{5,6},{6,7},{8,9},{9,10},{10,11},{12,13},{... | collective-permute-start | bytes 27656 | tf_op jit(solution)/shard_map/ppermute | solution.py:21
  299.8 6.4 collective-permute-start.11
  302.7 3.5 slice-start.2
  456.7 6.3 copy-start.6
  459.0 18.9 %collective-permute-start.14 = (f32[3,6,1,128]{3,0,2,1:T(4,128)S(1)}, f32[3,6,1,128]{3,0,2,1:T(4,128)S(1)}, u32[]{:S(2)}, u32[]{:S(2)}) collective-permute-start(f32[3,6,1,128]{3,0,2,1:T(4,128)S(1)} %slice.282), channel_id=1, source_target_pairs={{0,1},{1,2},{2,3},{4,5},{5,6},{6,7},{8,9},{9,10},{10,11},{12,13},{... | collective-permute-start | bytes 27656 | tf_op jit(solution)/shard_map/ppermute | solution.py:21
  460.3 17.6 %collective-permute-start.15 = (f32[3,6,1,128]{3,0,2,1:T(4,128)S(1)}, f32[3,6,1,128]{3,0,2,1:T(4,128)S(1)}, u32[]{:S(2)}, u32[]{:S(2)}) collective-permute-start(f32[3,6,1,128]{3,0,2,1:T(4,128)S(1)} %slice.285), channel_id=1, source_target_pairs={{1,0},{2,1},{3,2},{5,4},{6,5},{7,6},{9,8},{10,9},{11,10},{13,12},{... | collective-permute-start | bytes 27656 | tf_op jit(solution)/shard_map/ppermute | solution.py:21
  463.9 9.3 %collective-permute-start.12 = (f32[3,6,16,1]{3,0,2,1:T(4,128)}, f32[3,6,16,1]{3,0,2,1:T(4,128)}, u32[]{:S(2)}, u32[]{:S(2)}) collective-permute-start(f32[3,6,16,1]{3,0,2,1:T(4,128)} %slice.278), channel_id=1, source_target_pairs={{0,4},{4,8},{8,12},{12,0},{1,5},{5,9},{9,13},{13,1},{2,6},{6,10},{... | collective-permute-start | bytes 3464 | tf_op jit(solution)/shard_map/ppermute | solution.py:15
  466.7 11.1 %slice-start.4 = ((f32[3,6,16,128]{3,0,2,1:T(4,128)}), f32[3,6,15,128]{3,0,2,1:T(4,128)S(1)}, s32[]{:S(2)}) async-start(f32[3,6,16,128]{3,0,2,1:T(4,128)} %copy-done.6), calls=%async_computation.4 | async-start | bytes 368640 | tf_op jit(solution)/shard_map/slice | solution.py:65
  466.7 11.1 %collective-permute-start.13 = (f32[3,6,16,1]{3,0,2,1:T(4,128)S(1)}, f32[3,6,16,1]{3,0,2,1:T(4,128)}, u32[]{:S(2)}, u32[]{:S(2)}) collective-permute-start(f32[3,6,16,1]{3,0,2,1:T(4,128)S(1)} %bitcast.311), channel_id=1, source_target_pairs={{0,12},{4,0},{8,4},{12,8},{1,13},{5,1},{9,5},{13,9},{2,14},{6,2},{... | collective-permute-start | bytes 3464 | tf_op jit(solution)/shard_map/ppermute | solution.py:15
  662.6 9.2 %copy-start.2 = (f32[3,6,16,128]{3,0,2,1:T(4,128)}, f32[3,6,16,128]{3,0,2,1:T(4,128)S(1)}, u32[]{:S(2)}) copy-start(f32[3,6,16,128]{3,0,2,1:T(4,128)S(1)} %fusion.3) | copy-start | bytes 442372
  664.3 9.0 %collective-permute-start.16 = (f32[3,6,16,1]{3,0,2,1:T(4,128)S(1)}, f32[3,6,16,1]{3,0,2,1:T(4,128)S(1)}, u32[]{:S(2)}, u32[]{:S(2)}) collective-permute-start(f32[3,6,16,1]{3,0,2,1:T(4,128)S(1)} %slice.286), channel_id=1, source_target_pairs={{0,4},{4,8},{8,12},{12,0},{1,5},{5,9},{9,13},{13,1},{2,6},{6,10},{... | collective-permute-start | bytes 3464 | tf_op jit(solution)/shard_map/ppermute | solution.py:15
  666.4 8.5 %collective-permute-start.17 = (f32[3,6,16,1]{3,0,2,1:T(4,128)S(1)}, f32[3,6,16,1]{3,0,2,1:T(4,128)S(1)}, u32[]{:S(2)}, u32[]{:S(2)}) collective-permute-start(f32[3,6,16,1]{3,0,2,1:T(4,128)S(1)} %bitcast.318), channel_id=1, source_target_pairs={{0,12},{4,0},{8,4},{12,8},{1,13},{5,1},{9,5},{13,9},{2,14},{6,2},{... | collective-permute-start | bytes 3464 | tf_op jit(solution)/shard_map/ppermute | solution.py:15
  668.2 6.7 collective-permute-start.18
  669.5 5.4 collective-permute-start.19
  671.8 3.1 slice-start
where the time goes:
time: 687 us; the launch traced here: 677 us
  blocking collectives  533 us (78%)
  matrix products  47 us (7%)
  starting transfers between devices  32.2 us (5%)
  other arithmetic  24.7 us (4%)
  between operations  19.6 us (3%)
  local copies, waits for them, and re-layouts  13.2 us (2%)
  waiting for transfers between devices  7.07 us (1%)
    psum x10, blocking collectives, on_device(): height = lax.psum(jnp.sum(krylov[i] * candidate), ('circ', 'width'))  310 us
    psum x4, blocking collectives, on_device(): lax.psum(jnp.sum(candidate * candidate), ('circ', 'width'))  120 us
    all_gather x5, blocking collectives, coarse_sums(): return lax.all_gather(sector_sum[None, :], 'circ', axis=0, tiled=True)  38.7 us
    psum x1, blocking collectives, on_device(): lax.psum(jnp.sum(right_side * right_side), ('circ', 'width'))  35.5 us
    psum x5, blocking collectives, coarse_sums(): sector_sum = lax.psum(local_totals, 'width')  28.8 us
    dot_general x30, matrix products, transposed(): jnp.einsum('barw,brwc->arwc', coupling[d], vector, precision=highest)  28.7 us
    ppermute x10, starting transfers between devices, shifted(): return lax.ppermute(value, axis, pairs)  19.3 us
  transfers between devices with their start and end apart: 20, of which 3 were waited for; matrix products, arithmetic and copies ran while one was open for 3% of the time, Pallas kernels for 0%

commit v1 on v0

v1 whole, which is shorter than its diff:
```python
import functools

import jax
import jax.numpy as jnp
from jax import lax
from jax.experimental import pallas as pl
from jax.experimental.pallas import tpu as pltpu
from jax.sharding import PartitionSpec as P

ITERS = 4
MESH = pl.DeviceIdType.MESH
DIAGONAL = 54
JACOBI = 63
ROWS = 24


def repeat(count, body):
    if count <= 32:
        for step in range(count):
            body(step)
    else:
        lax.fori_loop(0, count, lambda step, carry: (body(step), carry)[1], 0)


def kernel(
    n_circ,
    n_width,
    forcing,
    case_ids,
    load_gain,
    stiffness,
    convection,
    labels,
    table,
    coarse_inverse,
    field_out,
    residual_out,
    coef,
    basis,
    image,
    padded,
    local,
    label_pad,
    solve_rows,
    ghost_x,
    ghost_w,
    stiff_x,
    stiff_w,
    send_dots,
    recv_dots,
    send_circ,
    recv_circ,
    send_width,
    recv_width,
    sem_send_dots,
    sem_recv_dots,
    sem_send_circ,
    sem_recv_circ,
    sem_send_width,
    sem_recv_width,
):
    layers, width, lanes = stiffness.shape
    slabs = 3 * layers
    group = n_circ * n_width
    at_circ = lax.axis_index("circ")
    at_width = lax.axis_index("width")
    me = at_circ * n_width + at_width
    next_circ = lax.rem(at_circ + 1, n_circ)
    prev_circ = lax.rem(at_circ + n_circ - 1, n_circ)
    next_width = lax.rem(at_width + 1, n_width)
    prev_width = lax.rem(at_width + n_width - 1, n_width)

    def other(step):
        place = lax.rem(me + step + 1, group)
        return {"circ": lax.div(place, n_width), "width": lax.rem(place, n_width)}

    barrier = pltpu.get_barrier_semaphore()
    repeat(
        group - 1,
        lambda step: pl.semaphore_signal(
            barrier, inc=1, device_id=other(step), device_id_type=MESH
        ),
    )

    lane = lax.broadcasted_iota(jnp.int32, (width, lanes), 1)
    even = lax.rem(lane, 2) == 0
    first = lane == 0
    last = lane == lanes - 1

    def roll(value, shift):
        return pltpu.roll(value, shift % lanes, 1)

    def splat(row):
        return jnp.broadcast_to(row, (width, lanes))

    def remote(source, target, send_sem, recv_sem, device):
        return pltpu.make_async_remote_copy(
            src_ref=source,
            dst_ref=target,
            send_sem=send_sem,
            recv_sem=recv_sem,
            device_id=device,
            device_id_type=MESH,
        )

    def neighbours(turn):
        rows = pl.ds(0, 64 if turn == 0 else ROWS)
        return [
            remote(
                send_width.at[turn, 0, rows],
                recv_width.at[turn, 0, rows],
                sem_send_width.at[turn, 0],
                sem_recv_width.at[turn, 0],
                {"circ": at_circ, "width": next_width},
            ),
            remote(
                send_width.at[turn, 1, rows],
                recv_width.at[turn, 1, rows],
                sem_send_width.at[turn, 1],
                sem_recv_width.at[turn, 1],
                {"circ": at_circ, "width": prev_width},
            ),
            remote(
                send_circ.at[turn],
                recv_circ.at[turn, 0],
                sem_send_circ.at[turn, 0],
                sem_recv_circ.at[turn, 0],
                {"circ": next_circ, "width": at_width},
            ),
            remote(
                send_circ.at[turn],
                recv_circ.at[turn, 1],
                sem_send_circ.at[turn, 1],
                sem_recv_circ.at[turn, 1],
                {"circ": prev_circ, "width": at_width},
            ),
        ]

    def send_all(turn, rows):
        message = jnp.concatenate(rows, axis=0)
        send_dots[turn] = message
        recv_dots[turn, me] = message
        repeat(
            group - 1,
            lambda step: remote(
                send_dots.at[turn],
                recv_dots.at[turn, me],
                sem_send_dots.at[turn],
                sem_recv_dots.at[turn],
                other(step),
            ).start(),
        )

    def all_wait(sem):
        whole = recv_dots.at[0, pl.ds(0, group - 1)]
        pltpu.make_async_copy(whole, whole, sem).wait()

    def total(values):
        acc = values[0]
        for value in values[1:]:
            acc = acc + value
        acc = acc[:8] + acc[8:]
        return jnp.sum(acc, axis=0, keepdims=True)

    nothing = jnp.zeros((1, lanes), jnp.float32)

    diagonal_mask = lax.broadcasted_iota(jnp.int32, (width, width), 0) == lax.broadcasted_iota(
        jnp.int32, (width, width), 1
    )
    label_all = labels[...].astype(jnp.float32)
    zone_lane = lane.astype(jnp.float32)
    zones = table.shape[0]

    def zone_rows(label):
        onehot = (label == zone_lane).astype(jnp.float32)[:, :zones]
        return jnp.dot(
            onehot, table[...], precision=lax.Precision.HIGHEST, preferred_element_type=jnp.float32
        )

    own_rows = []
    for r in range(layers):
        row = jnp.broadcast_to(label_all[r : r + 1], (width, width))
        column = jnp.sum(jnp.where(diagonal_mask, row, 0.0), axis=1, keepdims=True)
        label = jnp.broadcast_to(column, (width, lanes))
        label_pad[r, 8 : 8 + width] = label
        own_rows.append(zone_rows(label))
        for k in range(9):
            coef[JACOBI + k, r] = splat(own_rows[r][:, JACOBI + k : JACOBI + k + 1])

    def apply_jacobi(r, value):
        out = []
        for a in range(3):
            acc = coef[JACOBI + 3 * a, r] * value[0]
            for b in range(1, 3):
                acc = acc + coef[JACOBI + 3 * a + b, r] * value[b]
            out.append(acc)
        return out

    def pack(acc, index, value):
        return jnp.where(lax.div(lane, 2) == index, roll(value, 2 * index + 1), acc)

    def edges(turn, index, value):
        send_width[turn, 0, pl.ds(index, 1)] = value[width - 1 :]
        send_width[turn, 1, pl.ds(index, 1)] = value[:1]

    case = case_ids[0]
    load = [load_gain[case, a] for a in range(3)]
    sums = [[], [], []]
    packed = jnp.zeros((width, lanes), jnp.float32)
    for r in range(layers):
        value = [forcing[a, r] * load[a] for a in range(3)]
        mapped = apply_jacobi(r, value)
        for a in range(3):
            index = a * layers + r
            basis[0, index] = value[a]
            local[index] = mapped[a]
            sums[a].append(value[a])
            edges(0, index, mapped[a])
            packed = pack(packed, index, mapped[a])
        stiff = stiffness[r]
        ratio = 0.5 * convection[r] / stiff
        label = label_pad[r, 8 : 8 + width]
        packed = pack(packed, slabs + r, stiff)
        packed = pack(packed, slabs + layers + r, ratio)
        for a in range(3):
            edges(0, ROWS + a * layers + r, stiff)
        edges(0, 2 * ROWS + r, label)
    send_circ[0] = packed
    pl.semaphore_wait(barrier, group - 1)
    for copy in neighbours(0):
        copy.start()
    send_all(0, [nothing] * 5 + [total(sums[a]) for a in range(3)])

    for r in range(layers):
        for b in range(3):
            for a in range(3):
                k = 3 * b + a
                for d in (0, 1, 4, 5):
                    coef[9 * d + k, r] = -splat(own_rows[r][:, 9 * d + k : 9 * d + k + 1])
                own = splat(own_rows[r][:, DIAGONAL + k : DIAGONAL + k + 1])
                coef[DIAGONAL + k, r] = own + 7.0 if a == b else own
    order = 3 * n_circ
    for place, sector in enumerate((at_circ, prev_circ, next_circ)):
        for a in range(3):
            for k in range(order):
                scalar = coarse_inverse[sector * 3 + a, k]
                solve_rows[(place * 3 + a) * order + k] = jnp.full((8, lanes), scalar)

    norms = []
    heights = []
    for j in range(ITERS + 1):
        if j < ITERS:
            for copy in neighbours(j):
                copy.wait_recv()
        all_wait(sem_recv_dots.at[j])
        sectors = []
        for k in range(n_circ):
            acc = recv_dots[j, k * n_width]
            for w in range(1, n_width):
                acc = acc + recv_dots[j, k * n_width + w]
            sectors.append(jnp.broadcast_to(jnp.sum(acc, axis=1, keepdims=True), (8, lanes)))
        whole = sectors[0]
        for k in range(1, n_circ):
            whole = whole + sectors[k]

        def everywhere(array, q):
            return jnp.broadcast_to(array[q : q + 1], (8, lanes))

        if j > 0:
            norms.append(everywhere(whole, 4))
            column = [everywhere(whole, i) for i in range(j)]
            heights.append(column)
            shares = [column[i] / norms[i] for i in range(j)]
            wide = [jnp.concatenate([share, share], axis=0) for share in shares]
        else:
            wide = []
        if j == ITERS:
            square = everywhere(whole, 5)
            break

        parts = [everywhere(sectors[k], 5 + a) for k in range(n_circ) for a in range(3)]
        solved = []
        for place in range(3):
            for a in range(3):
                acc = solve_rows[(place * 3 + a) * order] * parts[0]
                for k in range(1, order):
                    acc = acc + solve_rows[(place * 3 + a) * order + k] * parts[k]
                solved.append(jnp.concatenate([acc, acc], axis=0))
        own_y, prev_y, next_y = solved[:3], solved[3:6], solved[6:]

        behind = recv_circ[j, 0]
        ahead = recv_circ[j, 1]
        halo = jnp.where(even, roll(ahead, -1), roll(behind, 1))
        span = 2 * layers
        if j == 0:
            stiff_x[...] = jnp.where(
                lane < span,
                roll(halo, -3 * span),
                jnp.where(lane < 2 * span, roll(halo, -2 * span), roll(halo, -span)),
            )
            for r in range(layers):
                ratio = 0.5 * convection[r] / stiffness[r]
                end = roll(halo, -(2 * (slabs + layers + r) + 1))
                low = jnp.where(first, end, roll(ratio, 1))
                high = jnp.where(last, end, roll(ratio, -1))
                for a in range(3):
                    coef[4 * a, r] = coef[4 * a, r] + low
                    coef[9 + 4 * a, r] = coef[9 + 4 * a, r] - high
        spread = [jnp.where(even, next_y[a], prev_y[a]) for a in range(3)]
        spread = jnp.where(
            lane < span, spread[0], jnp.where(lane < 2 * span, spread[1], spread[2])
        )
        halo = halo + stiff_x[...] * spread
        for i in range(j):
            halo = halo - wide[i] * ghost_x[i]
        ghost_x[j] = halo

        row_at = lax.broadcasted_iota(jnp.int32, (ROWS, lanes), 0)
        tall_y = [jnp.broadcast_to(own_y[a][:1], (ROWS, lanes)) for a in range(3)]
        row_y = jnp.where(
            row_at < layers, tall_y[0], jnp.where(row_at < 2 * layers, tall_y[1], tall_y[2])
        )
        for side in range(2):
            if j == 0:
                stiff_w[side] = recv_width[0, side, ROWS : 2 * ROWS]
                inside = at_width > 0 if side == 0 else at_width < n_width - 1
                end = jnp.where(inside, recv_width[0, side, 2 * ROWS : 2 * ROWS + 8], -1.0)
                for r in range(layers):
                    if side == 0:
                        label_pad[r, 7:8] = end[r : r + 1]
                    else:
                        label_pad[r, 8 + width : 9 + width] = end[r : r + 1]
            halo = recv_width[j, side, :ROWS] + stiff_w[side] * row_y
            for i in range(j):
                halo = halo - jnp.concatenate([shares[i]] * 3, axis=0) * ghost_w[i, side]
            ghost_w[j, side] = halo
            for index in range(slabs):
                if side == 0:
                    padded[j, index, 7:8] = halo[index : index + 1]
                else:
                    padded[j, index, 8 + width : 9 + width] = halo[index : index + 1]
        if j == 0:
            for r in range(layers):
                below = zone_rows(label_pad[r, 7 : 7 + width])
                above = zone_rows(label_pad[r, 9 : 9 + width])
                for k in range(9):
                    coef[18 + k, r] = -splat(below[:, 18 + k : 19 + k])
                    coef[27 + k, r] = -splat(above[:, 27 + k : 28 + k])

        squares = []
        for r in range(layers):
            stiff = stiffness[r]
            for a in range(3):
                index = a * layers + r
                value = local[index] + stiff * own_y[a]
                for i in range(j):
                    value = value - wide[i] * padded[i, index, 8 : 8 + width]
                padded[j, index, 8 : 8 + width] = value
                if j > 0:
                    vector = image[j - 1, index]
                    for i in range(j):
                        vector = vector - wide[i] * basis[i, index]
                    basis[j, index] = vector
                else:
                    vector = basis[0, index]
                squares.append(vector * vector)

        halo = ghost_x[j]
        products = [[] for i in range(j + 1)]
        lengths = []
        sums = [[], [], []]
        packed = jnp.zeros((width, lanes), jnp.float32)
        for r in range(layers):
            terms = []
            for b in range(3):
                index = b * layers + r
                value = padded[j, index, 8 : 8 + width]
                end = roll(halo, -(2 * index + 1))
                terms.append((DIAGONAL, r, b, value))
                terms.append((0, r, b, jnp.where(first, end, roll(value, 1))))
                terms.append((9, r, b, jnp.where(last, end, roll(value, -1))))
                terms.append((18, r, b, padded[j, index, 7 : 7 + width]))
                terms.append((27, r, b, padded[j, index, 9 : 9 + width]))
                if r > 0:
                    terms.append((36, r - 1, b, padded[j, index - 1, 8 : 8 + width]))
                if r < layers - 1:
                    terms.append((45, r + 1, b, padded[j, index + 1, 8 : 8 + width]))
            out = []
            for a in range(3):
                acc = None
                for base, layer, b, value in terms:
                    term = coef[base + 3 * b + a, layer] * value
                    acc = term if acc is None else acc + term
                out.append(acc)
                image[j, a * layers + r] = acc
                for i in range(j + 1):
                    products[i].append(basis[i, a * layers + r] * acc)
                if j == ITERS - 1:
                    lengths.append(acc * acc)
                else:
                    sums[a].append(acc)
            if j < ITERS - 1:
                mapped = apply_jacobi(r, out)
                for a in range(3):
                    index = a * layers + r
                    local[index] = mapped[a]
                    edges(j + 1, index, mapped[a])
                    packed = pack(packed, index, mapped[a])
        if j < ITERS - 1:
            send_circ[j + 1] = packed
            for copy in neighbours(j + 1):
                copy.start()
        rows = [total(product) for product in products]
        rows = rows + [nothing] * (4 - len(rows)) + [total(squares)]
        if j < ITERS - 1:
            rows = rows + [total(sums[a]) for a in range(3)]
        else:
            rows = rows + [total(lengths), nothing, nothing]
        send_all(j + 1, rows)

    sizes = [jnp.sqrt(norm) for norm in norms]
    rest = square
    for i in range(ITERS):
        rest = rest - heights[-1][i] * shares[i]
    rest = jnp.sqrt(jnp.maximum(rest, 0.0))
    rotated = [sizes[0]]
    rotations = []
    triangle = []
    for j in range(ITERS):
        column = [heights[j][i] / (sizes[i] * sizes[j]) for i in range(j + 1)]
        column.append((sizes[j + 1] if j + 1 < ITERS else rest) / sizes[j])
        for i in range(j):
            cosine, sine = rotations[i]
            top, low = column[i], column[i + 1]
            column[i] = cosine * top + sine * low
            column[i + 1] = cosine * low - sine * top
        radius = jnp.sqrt(column[j] * column[j] + column[j + 1] * column[j + 1])
        cosine, sine = column[j] / radius, column[j + 1] / radius
        rotations.append((cosine, sine))
        column[j] = radius
        carried = rotated[j]
        rotated[j] = cosine * carried
        rotated.append(-sine * carried)
        triangle.append(column[: j + 1])
    weights = [None] * ITERS
    for j in reversed(range(ITERS)):
        remainder = rotated[j]
        for k in range(j + 1, ITERS):
            remainder = remainder - triangle[k][j] * weights[k]
        weights[j] = remainder / triangle[j][j]
    wide = [weights[j] / sizes[j] for j in range(ITERS)]
    wide = [jnp.concatenate([weight, weight], axis=0) for weight in wide]
    for r in range(layers):
        inverse = 1.0 / stiffness[r]
        for a in range(3):
            index = a * layers + r
            value = wide[0] * padded[0, index, 8 : 8 + width]
            residual = basis[0, index] - wide[0] * image[0, index]
            for i in range(1, ITERS):
                value = value + wide[i] * padded[i, index, 8 : 8 + width]
                residual = residual - wide[i] * image[i, index]
            field_out[a, r] = value * inverse
            residual_out[a, r] = residual

    for turn in range(ITERS + 1):
        if turn < ITERS:
            for copy in neighbours(turn):
                copy.wait_send()
        all_wait(sem_send_dots.at[turn])


def on_device(
    n_circ,
    n_width,
    forcing,
    case_ids,
    load_gain,
    stiffness,
    convection,
    labels,
    zone_diagonal,
    zone_coupling,
    zone_jacobi,
    coarse_inverse,
):
    zones = zone_coupling.shape[0]
    table = jnp.concatenate(
        [
            zone_coupling.reshape(zones, 54),
            zone_diagonal.reshape(zones, 9),
            zone_jacobi.reshape(zones, 9),
        ],
        axis=1,
    )
    table = jnp.pad(table, ((0, 0), (0, 128 - table.shape[1])))
    layers, width, lanes = stiffness.shape
    slabs = 3 * layers
    group = n_circ * n_width
    f32 = jnp.float32
    in_vmem = pl.BlockSpec(memory_space=pltpu.VMEM)
    in_smem = pl.BlockSpec(memory_space=pltpu.SMEM)
    dma = pltpu.SemaphoreType.DMA
    return pl.pallas_call(
        functools.partial(kernel, n_circ, n_width),
        out_shape=(
            jax.ShapeDtypeStruct(forcing.shape, f32),
            jax.ShapeDtypeStruct(forcing.shape, f32),
        ),
        in_specs=[in_vmem, in_smem, in_smem, in_vmem, in_vmem, in_vmem, in_vmem, in_smem],
        out_specs=(in_vmem, in_vmem),
        scratch_shapes=[
            pltpu.VMEM((72, layers, width, lanes), f32),
            pltpu.VMEM((ITERS, slabs, width, lanes), f32),
            pltpu.VMEM((ITERS, slabs, width, lanes), f32),
            pltpu.VMEM((ITERS, slabs, width + 16, lanes), f32),
            pltpu.VMEM((slabs, width, lanes), f32),
            pltpu.VMEM((layers, width + 16, lanes), f32),
            pltpu.VMEM((9 * 3 * n_circ, 8, lanes), f32),
            pltpu.VMEM((ITERS, width, lanes), f32),
            pltpu.VMEM((ITERS, 2, ROWS, lanes), f32),
            pltpu.VMEM((width, lanes), f32),
            pltpu.VMEM((2, ROWS, lanes), f32),
            pltpu.VMEM((ITERS + 1, 8, lanes), f32),
            pltpu.VMEM((ITERS + 1, group, 8, lanes), f32),
            pltpu.VMEM((ITERS, width, lanes), f32),
            pltpu.VMEM((ITERS, 2, width, lanes), f32),
            pltpu.VMEM((ITERS, 2, 64, lanes), f32),
            pltpu.VMEM((ITERS, 2, 64, lanes), f32),
            dma((ITERS + 1,)),
            dma((ITERS + 1,)),
            dma((ITERS, 2)),
            dma((ITERS, 2)),
            dma((ITERS, 2)),
            dma((ITERS, 2)),
        ],
        compiler_params=pltpu.CompilerParams(
            collective_id=0, has_side_effects=True, vmem_limit_bytes=40 * 1024 * 1024
        ),
    )(forcing, case_ids, load_gain, stiffness, convection, labels, table, coarse_inverse)


def solution(mesh):
    return jax.shard_map(
        functools.partial(on_device, mesh.shape["circ"], mesh.shape["width"]),
        mesh=mesh,
        in_specs=(
            P(None, "cases", "width", "circ"),
            P("cases"),
            P(),
            P(None, "width", "circ"),
            P(None, "width", "circ"),
            P(None, "width"),
            P(),
            P(),
            P(),
            P(),
        ),
        out_specs=(P(None, "cases", "width", "circ"), P(None, "cases", "width", "circ")),
        check_vma=False,
    )
```

time: 687 us -> 39.7 us (0.06); the launches traced: 677 us -> 39.3 us
  blocking collectives: 533 us -> 0 us
  matrix products: 47 us -> 0 us
  starting transfers between devices: 32.2 us -> 0 us
  Pallas kernels: 0 us -> 31.9 us
  other arithmetic: 24.7 us -> 0.08 us
  between operations: 19.6 us -> 1.35 us
  local copies, waits for them, and re-layouts: 13.2 us -> 5.99 us
  waiting for transfers between devices: 7.07 us -> 0 us
    psum x20 -> x0, blocking collectives: 495 us -> none  [the longest x10 310 us: on_device(): height = lax.psum(jnp.sum(krylov[i] * candidate), ('circ', 'width'))]
    dot_general x48 -> x0, matrix products: 47 us -> none  [the longest x30 28.7 us: transposed(): jnp.einsum('barw,brwc->arwc', coupling[d], vector, precision=highest)]
    all_gather x5 -> x0, blocking collectives: 38.7 us -> none  [coarse_sums(): return lax.all_gather(sector_sum[None, :], 'circ', axis=0, tiled=True)]
    ppermute x20 -> x0, starting transfers between devices: 32.2 us -> none  [the longest x10 19.3 us: shifted(): return lax.ppermute(value, axis, pairs)]
    pallas_call x0 -> x1, Pallas kernels: none -> 31.9 us  [on_device(): pl.pallas_call(functools.partial(kernel, n_circ, n_width), out_shape=(jax...]
    reduce_sum x17 -> x0, other arithmetic: 21.3 us -> none  [the longest x6 9.55 us: on_device(): height = lax.psum(jnp.sum(krylov[i] * candidate), ('circ', 'width'))]
    slice x36 -> x0, local copies, waits for them, and re-layouts: 7.34 us -> none  [the longest x5 2.87 us: transposed(): contrib[3][:, :, 1:, :]]
    ppermute x20 -> x0, waiting for transfers between devices: 7.07 us -> none  [the longest x10 7.05 us: shifted(): return lax.ppermute(value, axis, pairs)]
  transfers between devices with their start and end apart: 20 -> 0, of which waited for: 3 -> 0; matrix products, arithmetic and copies ran while one was open for 3% -> 0% of each run, Pallas kernels for 0% -> 0%
where the time goes in v1:
time: 39.7 us; the launch traced here: 39.3 us
  Pallas kernels  31.9 us (80%)
  local copies, waits for them, and re-layouts  5.99 us (15%)
  between operations  1.35 us (3%)
    pallas_call x1, Pallas kernels, on_device(): pl.pallas_call(functools.partial(kernel, n_circ, n_width), out_shape=(jax...  31.9 us
    unnamed x14, local copies, waits for them, and re-layouts  4.34 us

profile of v1, /device:TPU:0, one launch (start us, length us, event | category | flops | bytes accessed | tf_op | source)
XLA Modules:
  0.0 39.3 jit_solution(3063415490593966703)
XLA Ops:
  0.6 0.0 copy-start
  1.3 0.8 %copy.20.load_gain = f32[16,3]{1,0:T(8,128)S(1)} copy(f32[16,3]{0,1:T(4,128)} %param.12) | data formatting | bytes 384 | tf_op args[2]
  2.1 0.7 %reshape.14 = f32[8,9]{0,1:T(8,128)S(1)} reshape(f32[8,3,3]{0,2,1:T(4,128)} %param.16) | data formatting | bytes 576 | tf_op jit(solution)/shard_map/reshape | solution.py:490
  2.8 0.1 copy.18
  2.9 0.7 %reshape.15 = f32[8,9]{0,1:T(8,128)S(1)} reshape(f32[8,3,3]{0,2,1:T(4,128)} %param.18) | data formatting | bytes 576 | tf_op jit(solution)/shard_map/reshape | solution.py:491
  3.6 0.1 copy.19
  3.6 0.9 %copy.16 = f32[8,6,3,3]{0,3,2,1:T(4,128)S(1)} copy(f32[8,6,3,3]{1,0,3,2:T(8,128)} %param.17) | data formatting | bytes 3456 | tf_op args[7]
  4.6 0.0 copy-start.1
  4.6 0.0 copy-start.2
  4.6 0.1 copy.17
  4.7 0.0 copy-start.4
  4.7 0.1 select_maximum_fusion.table
  4.7 0.0 copy-done
  4.7 0.6 %copy-done.1 = f32[6,16,128]{2,1,0:T(8,128)S(1)} copy-done((f32[6,16,128]{2,1,0:T(8,128)S(1)}, f32[6,16,128]{2,1,0:T(8,128)}, u32[]{:S(2)}) %copy-start.1) | copy-done | bytes 49176
  5.4 0.0 copy-done.2
  5.4 0.0 copy-done.4
  5.4 0.0 copy-start.3
  5.4 0.7 %copy-done.3 = f32[12,12]{1,0:T(8,128)S(1)} copy-done((f32[12,12]{1,0:T(8,128)S(1)}, f32[12,12]{1,0:T(8,128)}, u32[]{:S(2)}) %copy-start.3) | copy-done | bytes 600
  6.1 31.9 %shard_map.113 = (f32[3,6,16,128]{3,2,1,0:T(8,128)S(1)}, f32[3,6,16,128]{3,2,1,0:T(8,128)S(1)}) custom-call(f32[3,6,16,128]{3,2,1,0:T(8,128)S(1)} %copy-done, s32[1]{0:T(128)S(6)} %copy.23.case_ids, f32[16,3]{1,0:T(8,128)S(1)} %copy.20.load_gain, f32[6,16,128]{2,1,0:T(8,128)S(1)} %copy-done.1, f32[6,16,128]{2,1,0:T(8,128)S(1)} %copy-done.2, ...), custom_call_target="tpu_custom_call" | custom-call | tf_op jit(solution)/shard_map/pallas_call | solution.py:503
  37.9 0.7 %copy.24 = f32[3,6,16,128]{3,2,1,0:T(8,128)} copy(f32[3,6,16,128]{3,2,1,0:T(8,128)S(1)} %get-tuple-element.4) | data formatting | bytes 294912
  38.6 0.7 %copy.25 = f32[3,6,16,128]{3,2,1,0:T(8,128)} copy(f32[3,6,16,128]{3,2,1,0:T(8,128)S(1)} %get-tuple-element.5) | data formatting | bytes 294912
  (1 shorter events, 0.0 us)
Async XLA Ops:
  0.6 4.1 %copy-start = (f32[3,6,16,128]{3,2,1,0:T(8,128)S(1)}, f32[3,6,16,128]{3,2,1,0:T(8,128)}, u32[]{:S(2)}) copy-start(f32[3,6,16,128]{3,2,1,0:T(8,128)} %forcing.1) | copy-start | bytes 442372
  4.6 0.8 %copy-start.1 = (f32[6,16,128]{2,1,0:T(8,128)S(1)}, f32[6,16,128]{2,1,0:T(8,128)}, u32[]{:S(2)}) copy-start(f32[6,16,128]{2,1,0:T(8,128)} %stiffness.1) | copy-start | bytes 147460
  4.6 0.8 %copy-start.2 = (f32[6,16,128]{2,1,0:T(8,128)S(1)}, f32[6,16,128]{2,1,0:T(8,128)}, u32[]{:S(2)}) copy-start(f32[6,16,128]{2,1,0:T(8,128)} %convection.1) | copy-start | bytes 147460
  4.7 0.7 %copy-start.4 = (s32[6,16]{1,0:T(8,128)S(1)}, s32[6,16]{1,0:T(8,128)}, u32[]{:S(2)}) copy-start(s32[6,16]{1,0:T(8,128)} %labels.1) | copy-start | bytes 1156
  5.4 0.7 %copy-start.3 = (f32[12,12]{1,0:T(8,128)S(1)}, f32[12,12]{1,0:T(8,128)}, u32[]{:S(2)}) copy-start(f32[12,12]{1,0:T(8,128)} %coarse_inverse.1) | copy-start | bytes 1732

commit v2 on v1

--- a/solution.py
+++ b/solution.py
@@ -14,27 +14,32 @@
 ROWS = 24
 
 
-def repeat(count, body):
-    if count <= 32:
-        for step in range(count):
-            body(step)
-    else:
-        lax.fori_loop(0, count, lambda step, carry: (body(step), carry)[1], 0)
-
-
 def kernel(
     n_circ,
     n_width,
+    forcing_in,
+    case_in,
+    gain_in,
+    stiffness_in,
+    convection_in,
+    labels_in,
+    diagonal_in,
+    coupling_in,
+    jacobi_in,
+    coarse_in,
+    field_out,
+    residual_out,
     forcing,
     case_ids,
-    load_gain,
+    gain,
     stiffness,
     convection,
     labels,
-    table,
+    zone_diagonal,
+    zone_coupling,
+    zone_jacobi,
     coarse_inverse,
-    field_out,
-    residual_out,
+    sem_load,
     coef,
     basis,
     image,
@@ -70,17 +75,56 @@
     next_width = lax.rem(at_width + 1, n_width)
     prev_width = lax.rem(at_width + n_width - 1, n_width)
 
-    def other(step):
-        place = lax.rem(me + step + 1, group)
-        return {"circ": lax.div(place, n_width), "width": lax.rem(place, n_width)}
+    def far(count):
+        return sorted(range(count), key=lambda d: -min(d, count - d))
+
+    hops = [(d, e) for d in far(n_circ) for e in far(n_width) if d + e > 0]
+
+    def to_others(body):
+        if group <= 32:
+            for d, e in hops:
+                body(
+                    {
+                        "circ": lax.rem(at_circ + d, n_circ),
+                        "width": lax.rem(at_width + e, n_width),
+                    }
+                )
+        else:
+
+            def step(at, carry):
+                place = lax.rem(me + at + 1, group)
+                body({"circ": lax.div(place, n_width), "width": lax.rem(place, n_width)})
+                return carry
+
+            lax.fori_loop(0, group - 1, step, 0)
 
     barrier = pltpu.get_barrier_semaphore()
-    repeat(
-        group - 1,
-        lambda step: pl.semaphore_signal(
-            barrier, inc=1, device_id=other(step), device_id_type=MESH
-        ),
+    loads = [
+        pltpu.make_async_copy(source, target, sem_load.at[i])
+        for i, (source, target) in enumerate(
+            [
+                (labels_in, labels),
+                (jacobi_in, zone_jacobi),
+                (coupling_in, zone_coupling),
+                (diagonal_in, zone_diagonal),
+                (case_in, case_ids),
+                (gain_in, gain),
+                (forcing_in, forcing),
+                (stiffness_in, stiffness),
+                (convection_in, convection),
+                (coarse_in, coarse_inverse),
+            ]
+        )
+    ]
+    for copy in loads:
+        copy.start()
+    to_others(
+        lambda device: pl.semaphore_signal(
+            barrier, inc=1, device_id=device, device_id_type=MESH
+        )
     )
+    for copy in loads:
+        copy.wait()
 
     lane = lax.broadcasted_iota(jnp.int32, (width, lanes), 1)
     even = lax.rem(lane, 2) == 0
@@ -140,15 +184,14 @@
         message = jnp.concatenate(rows, axis=0)
         send_dots[turn] = message
         recv_dots[turn, me] = message
-        repeat(
-            group - 1,
-            lambda step: remote(
+        to_others(
+            lambda device: remote(
                 send_dots.at[turn],
                 recv_dots.at[turn, me],
                 sem_send_dots.at[turn],
                 sem_recv_dots.at[turn],
-                other(step),
-            ).start(),
+                device,
+            ).start()
         )
 
     def all_wait(sem):
@@ -169,13 +212,30 @@
     )
     label_all = labels[...].astype(jnp.float32)
     zone_lane = lane.astype(jnp.float32)
-    zones = table.shape[0]
+    zones, steps = zone_coupling.shape[2:]
+    table = jnp.concatenate(
+        [zone_coupling[b, a] for b in range(3) for a in range(3)], axis=1
+    )
 
     def zone_rows(label):
         onehot = (label == zone_lane).astype(jnp.float32)[:, :zones]
         return jnp.dot(
-            onehot, table[...], precision=lax.Precision.HIGHEST, preferred_element_type=jnp.float32
+            onehot, table, precision=lax.Precision.HIGHEST, preferred_element_type=jnp.float32
         )
+
+    def zone_columns(label, source):
+        onehot = (label == zone_lane).astype(jnp.float32)[:, :zones]
+        out = []
+        for p in range(3):
+            rows = lax.dot_general(
+                onehot,
+                source[p],
+                (((1,), (1,)), ((), ())),
+                precision=lax.Precision.HIGHEST,
+                preferred_element_type=jnp.float32,
+            )
+            out.extend(splat(rows[:, q : q + 1]) for q in range(3))
+        return out
 
     own_rows = []
     for r in range(layers):
@@ -184,8 +244,8 @@
         label = jnp.broadcast_to(column, (width, lanes))
         label_pad[r, 8 : 8 + width] = label
         own_rows.append(zone_rows(label))
-        for k in range(9):
-            coef[JACOBI + k, r] = splat(own_rows[r][:, JACOBI + k : JACOBI + k + 1])
+        for k, value in enumerate(zone_columns(label, zone_jacobi)):
+            coef[JACOBI + k, r] = value
 
     def apply_jacobi(r, value):
         out = []
@@ -204,7 +264,11 @@
         send_width[turn, 1, pl.ds(index, 1)] = value[:1]
 
     case = case_ids[0]
-    load = [load_gain[case, a] for a in range(3)]
+    chosen = jnp.where(
+        lax.broadcasted_iota(jnp.int32, gain.shape, 1) == case, gain[...], 0.0
+    )
+    chosen = jnp.sum(chosen, axis=1, keepdims=True)
+    load = [jnp.broadcast_to(chosen[a : a + 1], (width, lanes)) for a in range(3)]
     sums = [[], [], []]
     packed = jnp.zeros((width, lanes), jnp.float32)
     for r in range(layers):
@@ -232,19 +296,23 @@
     send_all(0, [nothing] * 5 + [total(sums[a]) for a in range(3)])
 
     for r in range(layers):
+        diagonal = zone_columns(label_pad[r, 8 : 8 + width], zone_diagonal)
         for b in range(3):
             for a in range(3):
                 k = 3 * b + a
                 for d in (0, 1, 4, 5):
-                    coef[9 * d + k, r] = -splat(own_rows[r][:, 9 * d + k : 9 * d + k + 1])
-                own = splat(own_rows[r][:, DIAGONAL + k : DIAGONAL + k + 1])
+                    coef[9 * d + k, r] = -splat(own_rows[r][:, steps * k + d : steps * k + d + 1])
+                own = diagonal[k]
                 coef[DIAGONAL + k, r] = own + 7.0 if a == b else own
     order = 3 * n_circ
     for place, sector in enumerate((at_circ, prev_circ, next_circ)):
         for a in range(3):
+            row = coarse_inverse[pl.ds(sector * 3 + a, 1)]
+            row = jnp.broadcast_to(row, (8, order))
             for k in range(order):
-                scalar = coarse_inverse[sector * 3 + a, k]
-                solve_rows[(place * 3 + a) * order + k] = jnp.full((8, lanes), scalar)
+                solve_rows[(place * 3 + a) * order + k] = jnp.broadcast_to(
+                    row[:, k : k + 1], (8, lanes)
+                )
 
     norms = []
     heights = []
@@ -344,8 +412,8 @@
                 below = zone_rows(label_pad[r, 7 : 7 + width])
                 above = zone_rows(label_pad[r, 9 : 9 + width])
                 for k in range(9):
-                    coef[18 + k, r] = -splat(below[:, 18 + k : 19 + k])
-                    coef[27 + k, r] = -splat(above[:, 27 + k : 28 + k])
+                    coef[18 + k, r] = -splat(below[:, steps * k + 2 : steps * k + 3])
+                    coef[27 + k, r] = -splat(above[:, steps * k + 3 : steps * k + 4])
 
         squares = []
         for r in range(layers):
@@ -483,32 +551,43 @@
     zone_jacobi,
     coarse_inverse,
 ):
-    zones = zone_coupling.shape[0]
-    table = jnp.concatenate(
-        [
-            zone_coupling.reshape(zones, 54),
-            zone_diagonal.reshape(zones, 9),
-            zone_jacobi.reshape(zones, 9),
-        ],
-        axis=1,
-    )
-    table = jnp.pad(table, ((0, 0), (0, 128 - table.shape[1])))
+    operands = [
+        forcing,
+        case_ids,
+        load_gain.T,
+        stiffness,
+        convection,
+        labels,
+        zone_diagonal.transpose(1, 2, 0),
+        zone_coupling.transpose(2, 3, 0, 1),
+        zone_jacobi.transpose(1, 2, 0),
+        coarse_inverse,
+    ]
     layers, width, lanes = stiffness.shape
     slabs = 3 * layers
     group = n_circ * n_width
     f32 = jnp.float32
     in_vmem = pl.BlockSpec(memory_space=pltpu.VMEM)
-    in_smem = pl.BlockSpec(memory_space=pltpu.SMEM)
+    in_hbm = pl.BlockSpec(memory_space=pltpu.HBM)
     dma = pltpu.SemaphoreType.DMA
-    return pl.pallas_call(
+    operands = [
+        operand if i == 1 else pltpu.with_memory_space_constraint(operand, pltpu.HBM)
+        for i, operand in enumerate(operands)
+    ]
+    results = pl.pallas_call(
         functools.partial(kernel, n_circ, n_width),
         out_shape=(
             jax.ShapeDtypeStruct(forcing.shape, f32),
             jax.ShapeDtypeStruct(forcing.shape, f32),
         ),
-        in_specs=[in_vmem, in_smem, in_smem, in_vmem, in_vmem, in_vmem, in_vmem, in_smem],
+        in_specs=[in_hbm] * len(operands),
         out_specs=(in_vmem, in_vmem),
         scratch_shapes=[
+            (pltpu.SMEM if i == 1 else pltpu.VMEM)(operand.shape, operand.dtype)
+            for i, operand in enumerate(operands)
+        ]
+        + [
+            dma((len(operands),)),
             pltpu.VMEM((72, layers, width, lanes), f32),
             pltpu.VMEM((ITERS, slabs, width, lanes), f32),
             pltpu.VMEM((ITERS, slabs, width, lanes), f32),
@@ -536,7 +615,8 @@
         compiler_params=pltpu.CompilerParams(
             collective_id=0, has_side_effects=True, vmem_limit_bytes=40 * 1024 * 1024
         ),
-    )(forcing, case_ids, load_gain, stiffness, convection, labels, table, coarse_inverse)
+    )(*operands)
+    return results
 
 
 def solution(mesh):

time: 39.7 us -> 33.6 us (0.85)
  local copies, waits for them, and re-layouts: 5.99 us -> 1.32 us
  Pallas kernels: 31.9 us -> 30.9 us
    unnamed x14 -> x2, local copies, waits for them, and re-layouts: 4.34 us -> 1.32 us
    reshape x6 -> x0, local copies, waits for them, and re-layouts: 1.65 us -> none  [the longest x2 0.78 us: on_device(): zone_diagonal.reshape(zones, 9)]
    pallas_call x1, Pallas kernels: 31.9 us -> 30.9 us  [on_device(): pl.pallas_call(functools.partial(kernel, n_circ, n_width), out_shape=(jax...]
where the time goes in v2:
time: 33.6 us; the launch traced here: 33.5 us
  Pallas kernels  30.9 us (92%)
  local copies, waits for them, and re-layouts  1.32 us (4%)
  between operations  1.29 us (4%)
    pallas_call x1, Pallas kernels, on_device(): pl.pallas_call(functools.partial(kernel, n_circ, n_width), out_shape=(jax...  30.9 us
    unnamed x2, local copies, waits for them, and re-layouts  1.32 us

profile of v2, /device:TPU:0, one launch (start us, length us, event | category | flops | bytes accessed | tf_op | source)
XLA Modules:
  0.0 33.5 jit_solution(13433252732962219458)
XLA Ops:
  1.3 30.9 %shard_map.113 = (f32[3,6,16,128]{3,2,1,0:T(8,128)S(1)}, f32[3,6,16,128]{3,2,1,0:T(8,128)S(1)}) custom-call(f32[3,6,16,128]{3,2,1,0:T(8,128)} %forcing_in.1, s32[1]{0:T(128)S(6)} %copy.14.case_in, f32[3,16]{1,0:T(4,128)} %bitcast.7, f32[6,16,128]{2,1,0:T(8,128)} %stiffness_in.1, f32[6,16,128]{2,1,0:T(8,128)} %convection_in.1, s32[6,16]{1,0:T(8,128)} %labels_in.1, ...), custom_call_target="tpu_custom_call" | custom-call | tf_op jit(solution)/shard_map/pallas_call | solution.py:577
  32.1 0.7 %copy.15 = f32[3,6,16,128]{3,2,1,0:T(8,128)} copy(f32[3,6,16,128]{3,2,1,0:T(8,128)S(1)} %get-tuple-element.4) | data formatting | bytes 294912
  32.8 0.7 %copy.16 = f32[3,6,16,128]{3,2,1,0:T(8,128)} copy(f32[3,6,16,128]{3,2,1,0:T(8,128)S(1)} %get-tuple-element.5) | data formatting | bytes 294912

commit v3 on v2

--- a/solution.py
+++ b/solution.py
@@ -316,10 +316,69 @@
 
     norms = []
     heights = []
+    sizes = []
+    rotated = []
+    rotations = []
+    triangle = []
+
+    def rotate(j):
+        if j == 0:
+            rotated.append(sizes[0])
+        column = [heights[j][i] / (sizes[i] * sizes[j]) for i in range(j + 1)]
+        column.append(sizes[j + 1] / sizes[j])
+        for i in range(j):
+            cosine, sine = rotations[i]
+            top, low = column[i], column[i + 1]
+            column[i] = cosine * top + sine * low
+            column[i + 1] = cosine * low - sine * top
+        radius = jnp.sqrt(column[j] * column[j] + column[j + 1] * column[j + 1])
+        cosine, sine = column[j] / radius, column[j + 1] / radius
+        rotations.append((cosine, sine))
+        column[j] = radius
+        carried = rotated[j]
+        rotated[j] = cosine * carried
+        rotated.append(-sine * carried)
+        triangle.append(column[: j + 1])
+
     for j in range(ITERS + 1):
         if j < ITERS:
             for copy in neighbours(j):
                 copy.wait_recv()
+            behind = recv_circ[j, 0]
+            ahead = recv_circ[j, 1]
+            halo = jnp.where(even, roll(ahead, -1), roll(behind, 1))
+            span = 2 * layers
+            if j == 0:
+                stiff_x[...] = jnp.where(
+                    lane < span,
+                    roll(halo, -3 * span),
+                    jnp.where(lane < 2 * span, roll(halo, -2 * span), roll(halo, -span)),
+                )
+                for r in range(layers):
+                    ratio = 0.5 * convection[r] / stiffness[r]
+                    end = roll(halo, -(2 * (slabs + layers + r) + 1))
+                    low = jnp.where(first, end, roll(ratio, 1))
+                    high = jnp.where(last, end, roll(ratio, -1))
+                    for a in range(3):
+                        coef[4 * a, r] = coef[4 * a, r] + low
+                        coef[9 + 4 * a, r] = coef[9 + 4 * a, r] - high
+            if j == 0:
+                for side in range(2):
+                    stiff_w[side] = recv_width[0, side, ROWS : 2 * ROWS]
+                    inside = at_width > 0 if side == 0 else at_width < n_width - 1
+                    end = jnp.where(inside, recv_width[0, side, 2 * ROWS : 2 * ROWS + 8], -1.0)
+                    for r in range(layers):
+                        if side == 0:
+                            label_pad[r, 7:8] = end[r : r + 1]
+                        else:
+                            label_pad[r, 8 + width : 9 + width] = end[r : r + 1]
+            if j == 0:
+                for r in range(layers):
+                    below = zone_rows(label_pad[r, 7 : 7 + width])
+                    above = zone_rows(label_pad[r, 9 : 9 + width])
+                    for k in range(9):
+                        coef[18 + k, r] = -splat(below[:, steps * k + 2 : steps * k + 3])
+                        coef[27 + k, r] = -splat(above[:, steps * k + 3 : steps * k + 4])
         all_wait(sem_recv_dots.at[j])
         sectors = []
         for k in range(n_circ):
@@ -356,24 +415,6 @@
                 solved.append(jnp.concatenate([acc, acc], axis=0))
         own_y, prev_y, next_y = solved[:3], solved[3:6], solved[6:]
 
-        behind = recv_circ[j, 0]
-        ahead = recv_circ[j, 1]
-        halo = jnp.where(even, roll(ahead, -1), roll(behind, 1))
-        span = 2 * layers
-        if j == 0:
-            stiff_x[...] = jnp.where(
-                lane < span,
-                roll(halo, -3 * span),
-                jnp.where(lane < 2 * span, roll(halo, -2 * span), roll(halo, -span)),
-            )
-            for r in range(layers):
-                ratio = 0.5 * convection[r] / stiffness[r]
-                end = roll(halo, -(2 * (slabs + layers + r) + 1))
-                low = jnp.where(first, end, roll(ratio, 1))
-                high = jnp.where(last, end, roll(ratio, -1))
-                for a in range(3):
-                    coef[4 * a, r] = coef[4 * a, r] + low
-                    coef[9 + 4 * a, r] = coef[9 + 4 * a, r] - high
         spread = [jnp.where(even, next_y[a], prev_y[a]) for a in range(3)]
         spread = jnp.where(
             lane < span, spread[0], jnp.where(lane < 2 * span, spread[1], spread[2])
@@ -389,15 +430,6 @@
             row_at < layers, tall_y[0], jnp.where(row_at < 2 * layers, tall_y[1], tall_y[2])
         )
         for side in range(2):
-            if j == 0:
-                stiff_w[side] = recv_width[0, side, ROWS : 2 * ROWS]
-                inside = at_width > 0 if side == 0 else at_width < n_width - 1
-                end = jnp.where(inside, recv_width[0, side, 2 * ROWS : 2 * ROWS + 8], -1.0)
-                for r in range(layers):
-                    if side == 0:
-                        label_pad[r, 7:8] = end[r : r + 1]
-                    else:
-                        label_pad[r, 8 + width : 9 + width] = end[r : r + 1]
             halo = recv_width[j, side, :ROWS] + stiff_w[side] * row_y
             for i in range(j):
                 halo = halo - jnp.concatenate([shares[i]] * 3, axis=0) * ghost_w[i, side]
@@ -407,14 +439,6 @@
                     padded[j, index, 7:8] = halo[index : index + 1]
                 else:
                     padded[j, index, 8 + width : 9 + width] = halo[index : index + 1]
-        if j == 0:
-            for r in range(layers):
-                below = zone_rows(label_pad[r, 7 : 7 + width])
-                above = zone_rows(label_pad[r, 9 : 9 + width])
-                for k in range(9):
-                    coef[18 + k, r] = -splat(below[:, steps * k + 2 : steps * k + 3])
-                    coef[27 + k, r] = -splat(above[:, steps * k + 3 : steps * k + 4])
-
         squares = []
         for r in range(layers):
             stiff = stiffness[r]
@@ -476,8 +500,6 @@
                     packed = pack(packed, index, mapped[a])
         if j < ITERS - 1:
             send_circ[j + 1] = packed
-            for copy in neighbours(j + 1):
-                copy.start()
         rows = [total(product) for product in products]
         rows = rows + [nothing] * (4 - len(rows)) + [total(squares)]
         if j < ITERS - 1:
@@ -485,31 +507,21 @@
         else:
             rows = rows + [total(lengths), nothing, nothing]
         send_all(j + 1, rows)
-
-    sizes = [jnp.sqrt(norm) for norm in norms]
+        if j < ITERS - 1:
+            for copy in neighbours(j + 1):
+                copy.start()
+        if j > 0:
+            sizes.append(jnp.sqrt(norms[j - 1]))
+        if j > 1:
+            rotate(j - 2)
+
+    sizes.append(jnp.sqrt(norms[-1]))
     rest = square
     for i in range(ITERS):
         rest = rest - heights[-1][i] * shares[i]
-    rest = jnp.sqrt(jnp.maximum(rest, 0.0))
-    rotated = [sizes[0]]
-    rotations = []
-    triangle = []
-    for j in range(ITERS):
-        column = [heights[j][i] / (sizes[i] * sizes[j]) for i in range(j + 1)]
-        column.append((sizes[j + 1] if j + 1 < ITERS else rest) / sizes[j])
-        for i in range(j):
-            cosine, sine = rotations[i]
-            top, low = column[i], column[i + 1]
-            column[i] = cosine * top + sine * low
-            column[i + 1] = cosine * low - sine * top
-        radius = jnp.sqrt(column[j] * column[j] + column[j + 1] * column[j + 1])
-        cosine, sine = column[j] / radius, column[j + 1] / radius
-        rotations.append((cosine, sine))
-        column[j] = radius
-        carried = rotated[j]
-        rotated[j] = cosine * carried
-        rotated.append(-sine * carried)
-        triangle.append(column[: j + 1])
+    sizes.append(jnp.sqrt(jnp.maximum(rest, 0.0)))
+    for j in range(ITERS - 2, ITERS):
+        rotate(j)
     weights = [None] * ITERS
     for j in reversed(range(ITERS)):
         remainder = rotated[j]

time: 33.6 us -> 32.8 us (0.976)
  Pallas kernels: 30.9 us -> 30 us
    pallas_call x1, Pallas kernels: 30.9 us -> 30 us  [on_device(): pl.pallas_call(functools.partial(kernel, n_circ, n_width), out_shape=(jax...]
where the time goes in v3:
time: 32.8 us; the launch traced here: 32.6 us
  Pallas kernels  30 us (91%)
  local copies, waits for them, and re-layouts  1.32 us (4%)
  between operations  1.29 us (4%)
    pallas_call x1, Pallas kernels, on_device(): pl.pallas_call(functools.partial(kernel, n_circ, n_width), out_shape=(jax...  30 us
    unnamed x2, local copies, waits for them, and re-layouts  1.32 us

profile of v3, /device:TPU:0, one launch (start us, length us, event | category | flops | bytes accessed | tf_op | source)
XLA Modules:
  0.0 32.6 jit_solution(5577651052281815628)
XLA Ops:
  1.3 30.0 %shard_map.113 = (f32[3,6,16,128]{3,2,1,0:T(8,128)S(1)}, f32[3,6,16,128]{3,2,1,0:T(8,128)S(1)}) custom-call(f32[3,6,16,128]{3,2,1,0:T(8,128)} %forcing_in.1, s32[1]{0:T(128)S(6)} %copy.14.case_in, f32[3,16]{1,0:T(4,128)} %bitcast.7, f32[6,16,128]{2,1,0:T(8,128)} %stiffness_in.1, f32[6,16,128]{2,1,0:T(8,128)} %convection_in.1, s32[6,16]{1,0:T(8,128)} %labels_in.1, ...), custom_call_target="tpu_custom_call" | custom-call | tf_op jit(solution)/shard_map/pallas_call | solution.py:589
  31.3 0.7 %copy.15 = f32[3,6,16,128]{3,2,1,0:T(8,128)} copy(f32[3,6,16,128]{3,2,1,0:T(8,128)S(1)} %get-tuple-element.4) | data formatting | bytes 294912
  32.0 0.7 %copy.16 = f32[3,6,16,128]{3,2,1,0:T(8,128)} copy(f32[3,6,16,128]{3,2,1,0:T(8,128)S(1)} %get-tuple-element.5) | data formatting | bytes 294912
